TPU v7x, 32 devices: a whole 2x2x4 slice. The times are simulated.
32 devices in a mesh: groups: 2 (over x), tok: 16 (over z, y, core).
Axes of the slice: x: 2, y: 2, z: 4, core: 2. Of those that a mesh axis runs over, the one named last changes fastest.
Arguments:
- queries: bfloat16 [4, 3072, 2048], P('groups', 'tok'), parts along dimension 0, may hold values from -6 to 6
- keys: bfloat16 [4, 3072, 2048], P('groups', 'tok'), parts along dimension 0, may hold values from -6 to 6
- values: bfloat16 [4, 3072, 2048], P('groups', 'tok'), parts along dimension 0, may hold values from -6 to 6
- rates: float32 [4, 4, 3072], P('groups', None, 'tok'), parts along dimension 0, may hold values from 4 to 64
- fast_init: bfloat16 [256, 3, 2048], P('tok'), may hold values from -6 to 6
Outputs:
- outputs: bfloat16 [4, 3072, 2048], P('groups', 'tok'), parts along dimension 0
- final_weights: float32 [256, 6, 2048], P('tok', 'groups'), parts along dimension 1
There are 2 independent parts, one for each index of `groups`. A program takes and returns all parts, laid end to end along the dimension named above; an argument that names none is the same for every part. Nothing has to cross between parts.
All inputs are finite; a program needn't handle non-finite values.
Results may differ from a plain program's by a relative error of at most 0.0081.
Values may be sent and summed in bfloat16 or wider, within the bound.
A program may use at most 128 MiB of HBM per device.

v0:
```python
import jax
import jax.numpy as jnp
from jax import lax
from jax.sharding import PartitionSpec as P


def project(inputs, weight):
    scale = inputs.shape[2] ** (-0.5)
    return jnp.einsum("thd,fhd->thf", inputs, weight, preferred_element_type=jnp.float32) * scale


def apply_fast(inputs, weight_full, heads):
    tokens = inputs.shape[0]
    hidden = weight_full.shape[0]
    width = inputs.shape[1] // heads
    shaped = inputs.reshape(tokens, heads, width)
    weight = weight_full.reshape(hidden, 3, heads, width)
    first = project(shaped, weight[:, 0])
    second = project(shaped, weight[:, 1])
    gated = (jax.nn.silu(first) * second).astype(jnp.bfloat16)
    mixed = jnp.einsum(
        "thf,fhd->thd", gated, weight[:, 2], preferred_element_type=jnp.float32
    ) * hidden ** (-0.5)
    return mixed.astype(jnp.bfloat16).reshape(tokens, heads * width)


def gradients(keys_rows, scaled_values, weight_full, heads, count):
    tokens = keys_rows.shape[0]
    hidden = weight_full.shape[0]
    width = keys_rows.shape[1] // heads
    shaped = keys_rows.reshape(tokens, heads, width)
    part = weight_full.reshape(count, 3, heads, width)
    first = project(shaped, part[:, 0])
    second = project(shaped, part[:, 1])
    active = jax.nn.silu(first)
    gated = (active * second).astype(jnp.bfloat16)
    back = jnp.einsum(
        "thd,fhd->thf", scaled_values, part[:, 2], preferred_element_type=jnp.float32
    ) * hidden ** (-0.5)
    sigma = jax.nn.sigmoid(first)
    delta_one = (back * second * sigma * (1.0 + first * (1.0 - sigma))).astype(jnp.bfloat16)
    delta_three = (back * active).astype(jnp.bfloat16)
    grad_one = jnp.einsum(
        "thf,thd->fhd", delta_one, shaped, preferred_element_type=jnp.float32
    ) * width ** (-0.5)
    grad_three = jnp.einsum(
        "thf,thd->fhd", delta_three, shaped, preferred_element_type=jnp.float32
    ) * width ** (-0.5)
    grad_two = jnp.einsum(
        "thf,thd->fhd", gated, scaled_values, preferred_element_type=jnp.float32
    ) * hidden ** (-0.5)
    return jnp.stack([grad_one, grad_three, grad_two], axis=1).reshape(count, 3, heads * width)


def renorm(weight, grad, heads, factor):
    rows = weight.shape[0]
    width = weight.shape[2] // heads
    old = weight.reshape(rows, 3, heads, width)
    moved = old + factor * grad.reshape(rows, 3, heads, width)
    old_norm = jnp.sqrt(jnp.sum(old * old, axis=3, keepdims=True))
    new_norm = jnp.sqrt(jnp.sum(moved * moved, axis=3, keepdims=True) + 1e-06)
    return (moved * old_norm / new_norm).reshape(rows, 3, heads * width)


def scale_values(values_rows, rate_rows, heads):
    tokens = values_rows.shape[0]
    width = values_rows.shape[1] // heads
    shaped = values_rows.reshape(tokens, heads, width).astype(jnp.float32)
    return (jnp.transpose(rate_rows)[:, :, None] * shaped).astype(jnp.bfloat16)


def per_device(queries, keys, values, rates, fast_init):
    shards = lax.axis_size("tok")
    heads = rates.shape[1]
    local_rows = fast_init.shape[0]
    all_rows = local_rows * shards
    factor = (keys.shape[1] * shards) ** (-0.5)
    weight_zero = lax.all_gather(fast_init, "tok", axis=0, tiled=True)
    result_zero = apply_fast(queries[0], weight_zero, heads)
    scaled_zero = scale_values(values[0], rates[0], heads)
    summed = lax.psum(gradients(keys[0], scaled_zero, weight_zero, heads, all_rows), "tok")
    state_full = renorm(weight_zero.astype(jnp.float32), summed, heads, factor)
    weight_one = state_full.astype(jnp.bfloat16)
    state_one = lax.dynamic_slice_in_dim(
        state_full, lax.axis_index("tok") * local_rows, local_rows, 0
    )
    result_one = apply_fast(queries[1], weight_one, heads)
    scaled_one = scale_values(values[1], rates[1], heads)
    shares_two = lax.psum_scatter(
        gradients(keys[1], scaled_one, weight_one, heads, lax.axis_size("tok") * local_rows),
        "tok",
        scatter_dimension=0,
        tiled=True,
    )
    state_two = renorm(state_one, shares_two, heads, factor)
    return (jnp.stack([result_zero, result_one], axis=0), state_two)


def solution(mesh):
    in_specs = (
        P("groups", "tok", None),
        P("groups", "tok", None),
        P("groups", "tok", None),
        P("groups", None, "tok"),
        P("tok", None, None),
    )
    out_specs = (P("groups", "tok", None), P("tok", "groups", None))
    return jax.shard_map(
        per_device, mesh=mesh, in_specs=in_specs, out_specs=out_specs, check_vma=False
    )
```

profile of v0, /device:TPU:0, one launch (start us, length us, event | category | flops | bytes accessed | tf_op | source)
XLA Modules:
  0.0 452.2 jit_solution(16619257049928713187)
XLA Ops:
  15.7 42.4 %all-gather.2.cloned.1.call-done = bf16[256,3,2048]{2,0,1:T(8,128)(2,1)} async-done(((bf16[16,3,2048]{2,0,1:T(8,128)(2,1)}), bf16[256,3,2048]{2,0,1:T(8,128)(2,1)}) %all-gather.2.cloned.1.call-update) | async-done | bytes 3145744 | tf_op jit(solution)/shard_map/all_gather | solution.py:78
  58.1 3.2 copy.37
  71.7 2.9 copy.51
  74.7 2.9 copy.49
  77.6 5.9 %pad_maximum_fusion = f32[256,3,2048]{0,2,1:T(8,128)} fusion(f32[256,1,2048]{0,2,1:T(8,128)} %bitcast.139, f32[256,1,2048]{0,2,1:T(8,128)} %bitcast.130, f32[256,1,2048]{0,2,1:T(8,128)} %bitcast.132), kind=kLoop, calls=%fused_computation.2 | loop fusion | flops 3145728 | bytes 12582912 | tf_op jit(solution)/shard_map/stack | solution.py:52
  83.8 3.0 reshape_squeeze.17
  86.8 3.3 reshape.75
  90.1 131.4 %all-reduce.4.cloned.1.call-done = f32[256,3,2048]{0,2,1:T(8,128)} async-done(((f32[256,3,2048]{0,2,1:T(8,128)}), f32[256,3,2048]{0,2,1:T(8,128)}) %all-reduce.4.cloned.1.call-update) | async-done | bytes 6291472 | tf_op jit(solution)/shard_map/psum | solution.py:81
  221.5 4.4 bitcast_reduce_fusion.1
  226.1 4.0 fusion.70
  239.9 2.9 copy.64
  242.8 2.9 copy.62
  245.7 5.9 %pad_maximum_fusion.1 = f32[256,3,2048]{0,2,1:T(8,128)} fusion(f32[256,1,2048]{0,2,1:T(8,128)} %bitcast.140, f32[256,1,2048]{0,2,1:T(8,128)} %bitcast.131, f32[256,1,2048]{0,2,1:T(8,128)} %bitcast.133), kind=kLoop, calls=%fused_computation.3 | loop fusion | flops 3145728 | bytes 12582912 | tf_op jit(solution)/shard_map/stack | solution.py:52
  251.6 9.6 %copy.65 = f32[256,3,2048]{2,1,0:T(4,128)} copy(f32[256,3,2048]{0,2,1:T(8,128)} %pad_maximum_fusion.1) | data formatting | bytes 12582912 | tf_op jit(solution)/shard_map/stack | solution.py:52
  264.0 3.0 reshape_squeeze.16
  267.0 3.0 reshape_squeeze.14
  273.7 3.1 fusion.3
  276.8 2.8 copy.43
  279.5 2.8 stack_reshape.6
  285.1 3.1 fusion.4
  291.9 139.5 %all-reduce.6.cloned.1.call-done = f32[256,3,2048]{2,1,0:T(4,128)} async-done(((f32[256,3,2048]{2,1,0:T(4,128)}), f32[256,3,2048]{2,1,0:T(4,128)}) %all-reduce.6.cloned.1.call-update) | async-done | bytes 6291472
  435.3 2.9 bitcast_reduce_fusion.3
  438.3 4.4 bitcast_divide_fusion.1
  442.7 3.0 copy.67
  (58 shorter events, 45.2 us)
Async XLA Ops:
  7.2 4.8 %copy-start.6 = (bf16[2,192,2048]{2,1,0:T(8,128)(2,1)S(1)}, bf16[2,192,2048]{2,1,0:T(8,128)(2,1)}, u32[]{:S(2)}) copy-start(bf16[2,192,2048]{2,1,0:T(8,128)(2,1)} %param.7) | copy-start | bytes 4718596
  7.2 51.0 %all-gather.2.cloned.1.call-start = ((), (), s32[]{:S(2)}) async-start(), calls=%async_computation | async-start | bytes 3342336 | tf_op jit(solution)/shard_map/all_gather | solution.py:78
  7.9 213.6 %all-reduce.4.cloned.1.call-start = ((), (), s32[]{:S(2)}) async-start(), calls=%async_computation.1 | async-start | bytes 12582912 | tf_op jit(solution)/shard_map/psum | solution.py:81
  11.9 3.8 copy-start.9
  61.3 3.2 copy-start.2
  65.2 2.4 copy-start.8
  83.5 347.9 %all-reduce.6.cloned.1.call-start = ((), (), s32[]{:S(2)}) async-start(), calls=%async_computation.2 | async-start | bytes 16777216
  221.5 4.6 %copy-start = (f32[256,3,2048]{0,2,1:T(8,128)S(1)}, f32[256,3,2048]{0,2,1:T(8,128)}, u32[]{:S(2)}) copy-start(f32[256,3,2048]{0,2,1:T(8,128)} %all-reduce.4.cloned.1.call-done) | copy-start | bytes 18874372
  226.1 4.0 copy-start.7
  230.0 3.3 copy-start.3
  230.0 2.5 copy-start.1
  261.3 8.8 %copy-start.10 = (u32[32]{0:T(128)S(1)}, u32[32]{0:T(128)}, u32[]{:S(2)}) copy-start(u32[32]{0:T(128)} %constant.34) | copy-start | bytes 388
  276.8 8.3 %copy-start.4 = (bf16[256,3,2048]{0,2,1:T(8,128)(2,1)S(1)}, bf16[256,3,2048]{0,2,1:T(8,128)(2,1)}, u32[]{:S(2)}) copy-start(bf16[256,3,2048]{0,2,1:T(8,128)(2,1)} %copy-done.3) | copy-start | bytes 9437188
  288.2 2.4 copy-start.5
Sparse Core Ops, SparseCore 0:
  10.2 47.9 all-gather.1
  83.7 137.7 all-reduce.3
  261.4 169.9 all-reduce.5
where the time goes:
time: 453 us; the launch traced here: 452 us
  waiting for transfers between devices  314 us (69%)
  local copies, waits for them, and re-layouts  63.2 us (14%)
  other arithmetic  30.4 us (7%)
  matrix products  29.7 us (7%)
  between operations  14.6 us (3%)
    unnamed x4, waiting for transfers between devices  140 us
    psum x1, waiting for transfers between devices, per_device(): lax.psum(gradients(keys[0], scaled_zero, weight_zero, heads, all_rows), '...  131 us
    all_gather x1, waiting for transfers between devices, per_device(): weight_zero = lax.all_gather(fast_init, 'tok', axis=0, tiled=True)  42.4 us
    another operation x2, other arithmetic, gradients(): jnp.stack([grad_one, grad_three, grad_two], axis=1)  11.9 us
    another operation x1, local copies, waits for them, and re-layouts, gradients(): jnp.stack([grad_one, grad_three, grad_two], axis=1)  9.62 us
  transfers between devices with their start and end apart: 3, of which 3 were waited for; matrix products, arithmetic and copies ran while one was open for 10% of the time, Pallas kernels for 0%

commit v1 on v0

--- a/solution.py
+++ b/solution.py
@@ -1,6 +1,10 @@
+import functools
+
 import jax
 import jax.numpy as jnp
 from jax import lax
+from jax.experimental import pallas as pl
+from jax.experimental.pallas import tpu as pltpu
 from jax.sharding import PartitionSpec as P
 
 
@@ -69,7 +73,7 @@
     return (jnp.transpose(rate_rows)[:, :, None] * shaped).astype(jnp.bfloat16)
 
 
-def per_device(queries, keys, values, rates, fast_init):
+def per_device_plain(queries, keys, values, rates, fast_init):
     shards = lax.axis_size("tok")
     heads = rates.shape[1]
     local_rows = fast_init.shape[0]
@@ -96,6 +100,223 @@
     return (jnp.stack([result_zero, result_one], axis=0), state_two)
 
 
+def dot_nt(a, b):
+    return lax.dot_general(a, b, (((1,), (1,)), ((), ())), preferred_element_type=jnp.float32)
+
+
+def dot_nn(a, b):
+    return lax.dot_general(a, b, (((1,), (0,)), ((), ())), preferred_element_type=jnp.float32)
+
+
+def fused(
+    shards, heads, hidden, width, rows, factor,
+    q_ref, k_ref, v_ref, rate_ref, init_ref, out_ref, final_ref,
+    weights, acc, state, stage, landed, gather_send, gather_recv, sum_send, sum_recv,
+):
+    me = lax.axis_index("tok")
+    bits = shards.bit_length() - 1
+    bit = [lax.rem(me // (1 << p), 2) for p in range(bits)]
+    partner = [me + (1 << p) * (1 - 2 * bit[p]) for p in range(bits)]
+    spans = [hidden >> (p + 1) for p in range(bits)]
+    base = [0]
+    for p in range(bits):
+        base.append(base[p] + bit[p] * spans[p])
+    own = pl.multiple_of(base[bits], rows)
+    offset = [sum(spans[:p]) for p in range(bits)]
+
+    barrier = pltpu.get_barrier_semaphore()
+    for p in range(bits):
+        pl.semaphore_signal(
+            barrier, inc=1, device_id={"tok": partner[p]}, device_id_type=pl.DeviceIdType.MESH
+        )
+    pl.semaphore_wait(barrier, bits)
+
+    def gather_copy(block, p, h):
+        start = pl.multiple_of(base[p + 1], rows)
+        part = weights.at[block, h, pl.ds(start, spans[p]), :]
+        return pltpu.make_async_remote_copy(
+            src_ref=part,
+            dst_ref=part,
+            send_sem=gather_send.at[block, p, h],
+            recv_sem=gather_recv.at[block, p, h],
+            device_id={"tok": partner[p]},
+            device_id_type=pl.DeviceIdType.MESH,
+        )
+
+    def sum_copy(block, p, h):
+        return pltpu.make_async_remote_copy(
+            src_ref=stage.at[block, h, pl.ds(offset[p], spans[p]), :],
+            dst_ref=landed.at[block, h, pl.ds(offset[p], spans[p]), :],
+            send_sem=sum_send.at[block, p, h],
+            recv_sem=sum_recv.at[block, p, h],
+            device_id={"tok": partner[p]},
+            device_id_type=pl.DeviceIdType.MESH,
+        )
+
+    def columns(h):
+        return slice(h * width, (h + 1) * width)
+
+    def weight(block, h, m):
+        return weights[block, h, :, columns(m)]
+
+    wide = width ** (-0.5)
+    deep = hidden ** (-0.5)
+
+    def apply_head(block, h):
+        x = q_ref[block, :, columns(h)]
+        first = dot_nt(x, weight(block, h, 0)) * wide
+        second = dot_nt(x, weight(block, h, 1)) * wide
+        gated = (first / (1.0 + jnp.exp(-first)) * second).astype(jnp.bfloat16)
+        mixed = dot_nn(gated, weight(block, h, 2)) * deep
+        out_ref[block, :, columns(h)] = mixed.astype(jnp.bfloat16)
+
+    def gradient_head(block, h):
+        k = k_ref[block, :, columns(h)]
+        scaled = (rate_ref[block, :, h : h + 1] * v_ref[block, :, columns(h)].astype(jnp.float32)).astype(
+            jnp.bfloat16
+        )
+        first = dot_nt(weight(block, h, 0), k) * wide
+        second = dot_nt(weight(block, h, 1), k) * wide
+        back = dot_nt(weight(block, h, 2), scaled) * deep
+        sigma = 1.0 / (1.0 + jnp.exp(-first))
+        active = first * sigma
+        gated = (active * second).astype(jnp.bfloat16)
+        delta_one = (back * second * sigma * (1.0 + first * (1.0 - sigma))).astype(jnp.bfloat16)
+        delta_three = (back * active).astype(jnp.bfloat16)
+        acc[h, :, columns(0)] = dot_nn(delta_one, k)
+        acc[h, :, columns(1)] = dot_nn(delta_three, k)
+        acc[h, :, columns(2)] = dot_nn(gated, scaled)
+
+    def send_sum(block, p, h):
+        away = pl.multiple_of(base[p] + (1 - bit[p]) * spans[p], rows)
+        total = acc[h, pl.ds(away, spans[p]), :]
+        if p > 0:
+            before = pl.multiple_of(offset[p - 1] + (1 - bit[p]) * spans[p], rows)
+            total = total + landed[block, h, pl.ds(before, spans[p]), :].astype(jnp.float32)
+        stage[block, h, offset[p] : offset[p] + spans[p], :] = total.astype(jnp.bfloat16)
+        sum_copy(block, p, h).start()
+        if p > 0:
+            keep = pl.multiple_of(base[p + 1], rows)
+            before = pl.multiple_of(offset[p - 1] + bit[p] * spans[p], rows)
+            acc[h, pl.ds(keep, spans[p]), :] = acc[h, pl.ds(keep, spans[p]), :] + landed[
+                block, h, pl.ds(before, spans[p]), :
+            ].astype(jnp.float32)
+
+    def renorm_head(block, h):
+        last = bits - 1
+        for m, scale in enumerate((wide, wide, deep)):
+            grad = acc[h, pl.ds(own, rows), columns(m)] + landed[
+                block, h, offset[last] : offset[last] + rows, columns(m)
+            ].astype(jnp.float32)
+            if block == 0:
+                old = init_ref[h, :, columns(m)].astype(jnp.float32)
+            else:
+                old = state[h, :, columns(m)]
+            moved = old + (factor * scale) * grad
+            old_norm = jnp.sqrt(jnp.sum(old * old, axis=1, keepdims=True))
+            new_norm = jnp.sqrt(jnp.sum(moved * moved, axis=1, keepdims=True) + 1e-06)
+            fresh = moved * (old_norm / new_norm)
+            if block == 0:
+                state[h, :, columns(m)] = fresh
+                weights[1, h, pl.ds(own, rows), columns(m)] = fresh.astype(jnp.bfloat16)
+            else:
+                final_ref[h, :, columns(m)] = fresh
+
+    def gather_step(block, step, h):
+        p = bits - 1 - step
+        gather_copy(block, p, h).wait_recv()
+        if p > 0:
+            gather_copy(block, p - 1, h).start()
+
+    for h in range(heads):
+        weights[0, h, pl.ds(own, rows), :] = init_ref[h]
+        gather_copy(0, bits - 1, h).start()
+    for turn in range(heads + bits - 1):
+        for step in range(bits - 1, -1, -1):
+            h = turn - step
+            if 0 <= h < heads:
+                gather_step(0, step, h)
+                if step == bits - 1:
+                    gradient_head(0, h)
+                    send_sum(0, 0, h)
+    for turn in range(heads + bits - 1):
+        for p in range(bits - 1, -1, -1):
+            h = turn - p
+            if 0 <= h < heads:
+                sum_copy(0, p, h).wait_recv()
+                if p < bits - 1:
+                    send_sum(0, p + 1, h)
+                else:
+                    renorm_head(0, h)
+                    gather_copy(1, bits - 1, h).start()
+        if turn < heads:
+            apply_head(0, turn)
+    for turn in range(heads + bits - 1):
+        for step in range(bits - 1, -1, -1):
+            h = turn - step
+            if 0 <= h < heads:
+                gather_step(1, step, h)
+                if step == bits - 1:
+                    gradient_head(1, h)
+                    send_sum(1, 0, h)
+    for turn in range(heads + bits - 1):
+        for p in range(bits - 1, -1, -1):
+            h = turn - p
+            if 0 <= h < heads:
+                sum_copy(1, p, h).wait_recv()
+                if p < bits - 1:
+                    send_sum(1, p + 1, h)
+                else:
+                    renorm_head(1, h)
+        if turn < heads:
+            apply_head(1, turn)
+    for block in range(2):
+        for p in range(bits):
+            for h in range(heads):
+                gather_copy(block, p, h).wait_send()
+                sum_copy(block, p, h).wait_send()
+
+
+def per_device(queries, keys, values, rates, fast_init):
+    shards = lax.axis_size("tok")
+    heads = rates.shape[1]
+    rows = fast_init.shape[0]
+    if shards & (shards - 1) or rows % 16:
+        return per_device_plain(queries, keys, values, rates, fast_init)
+    bits = shards.bit_length() - 1
+    blocks, tokens, features = keys.shape
+    width = features // heads
+    hidden = rows * shards
+    factor = (tokens * shards) ** (-0.5)
+    start = fast_init.reshape(rows, 3, heads, width).transpose(2, 0, 1, 3).reshape(heads, rows, 3 * width)
+    vmem = pl.BlockSpec(memory_space=pltpu.VMEM)
+    outputs, final = pl.pallas_call(
+        functools.partial(fused, shards, heads, hidden, width, rows, factor),
+        out_shape=(
+            jax.ShapeDtypeStruct((blocks, tokens, features), jnp.bfloat16),
+            jax.ShapeDtypeStruct((heads, rows, 3 * width), jnp.float32),
+        ),
+        in_specs=[vmem] * 5,
+        out_specs=(vmem, vmem),
+        scratch_shapes=[
+            pltpu.VMEM((2, heads, hidden, 3 * width), jnp.bfloat16),
+            pltpu.VMEM((heads, hidden, 3 * width), jnp.float32),
+            pltpu.VMEM((heads, rows, 3 * width), jnp.float32),
+            pltpu.VMEM((2, heads, hidden - rows, 3 * width), jnp.bfloat16),
+            pltpu.VMEM((2, heads, hidden - rows, 3 * width), jnp.bfloat16),
+            pltpu.SemaphoreType.DMA((2, bits, heads)),
+            pltpu.SemaphoreType.DMA((2, bits, heads)),
+            pltpu.SemaphoreType.DMA((2, bits, heads)),
+            pltpu.SemaphoreType.DMA((2, bits, heads)),
+        ],
+        compiler_params=pltpu.CompilerParams(
+            collective_id=0, has_side_effects=True, vmem_limit_bytes=52 * 1024 * 1024
+        ),
+    )(queries, keys, values, jnp.transpose(rates, (0, 2, 1)), start)
+    final = final.reshape(heads, rows, 3, width).transpose(1, 2, 0, 3).reshape(rows, 3, features)
+    return outputs, final
+
+
 def solution(mesh):
     in_specs = (
         P("groups", "tok", None),

time: 453 us -> 139 us (0.31)
  waiting for transfers between devices: 314 us -> 0 us
  Pallas kernels: 0 us -> 133 us
  local copies, waits for them, and re-layouts: 63.2 us -> 5.04 us
  other arithmetic: 30.4 us -> 0 us
  matrix products: 29.7 us -> 0 us
  between operations: 14.6 us -> 0.68 us
    unnamed x4 -> x0, waiting for transfers between devices: 140 us -> none
    pallas_call x0 -> x1, Pallas kernels: none -> 133 us  [per_device(): pl.pallas_call(functools.partial(fused, shards, heads, hidden, width, row...]
    psum x1 -> x0, waiting for transfers between devices: 131 us -> none  [per_device(): lax.psum(gradients(keys[0], scaled_zero, weight_zero, heads, all_rows), '...]
    all_gather x1 -> x0, waiting for transfers between devices: 42.4 us -> none  [per_device(): weight_zero = lax.all_gather(fast_init, 'tok', axis=0, tiled=True)]
    dot_general x16 -> x0, matrix products: 29.7 us -> none  [the longest x6 9.06 us: project(): jnp.einsum('thd,fhd->thf', inputs, weight, preferred_element_type=jnp.flo...]
    another operation x7 -> x0, local copies, waits for them, and re-layouts: 23.5 us -> none  [the longest x1 9.62 us: gradients(): jnp.stack([grad_one, grad_three, grad_two], axis=1)]
    another operation x3 -> x0, other arithmetic: 13.1 us -> none  [the longest x2 11.9 us: gradients(): jnp.stack([grad_one, grad_three, grad_two], axis=1)]
    mul x4 -> x0, local copies, waits for them, and re-layouts: 11.7 us -> none  [the longest x2 5.85 us: gradients(): jnp.einsum('thf,thd->fhd', delta_three, shaped, preferred_element_type=jn...]
  transfers between devices with their start and end apart: 3 -> 0, of which waited for: 3 -> 0; matrix products, arithmetic and copies ran while one was open for 10% -> 0% of each run, Pallas kernels for 0% -> 0%
where the time goes in v1:
time: 139 us
  Pallas kernels  133 us (96%)
  local copies, waits for them, and re-layouts  5.04 us (4%)
    pallas_call x1, Pallas kernels, per_device(): pl.pallas_call(functools.partial(fused, shards, heads, hidden, width, row...  133 us

profile of v1, /device:TPU:0, one launch (start us, length us, event | category | flops | bytes accessed | tf_op | source)
XLA Modules:
  0.0 139.1 jit_solution(10003789858997633378)
XLA Ops:
  0.6 0.8 copy.12
  1.5 1.1 reshape.16
  2.5 0.2 copy.16
  2.7 0.3 reshape.17.init_ref
  3.0 133.4 %shard_map.68 = (bf16[2,192,2048]{2,1,0:T(8,128)(2,1)}, f32[4,16,1536]{2,1,0:T(8,128)S(1)}) custom-call(bf16[2,192,2048]{2,1,0:T(8,128)(2,1)} %q_ref.1, bf16[2,192,2048]{2,1,0:T(8,128)(2,1)} %k_ref.1, bf16[2,192,2048]{2,1,0:T(8,128)(2,1)} %v_ref.1, f32[2,192,4]{2,1,0:T(8,128)S(1)} %bitcast.9, bf16[4,16,1536]{2,1,0:T(8,128)(2,1)S(1)} %reshape.17.init_ref), custom_call_target="tpu_custom_call" | custom-call | tf_op jit(solution)/shard_map/pallas_call | solution.py:293
  136.4 0.0 copy-start
  136.4 0.3 reshape.18
  136.7 0.3 copy.14
  136.9 1.0 reshape.19
  138.0 0.0 copy-done
  138.0 1.1 copy.18
Async XLA Ops:
  136.4 1.6 %copy-start = (bf16[2,192,2048]{2,1,0:T(8,128)(2,1)S(1)}, bf16[2,192,2048]{2,1,0:T(8,128)(2,1)}, u32[]{:S(2)}) copy-start(bf16[2,192,2048]{2,1,0:T(8,128)(2,1)} %get-tuple-element.8) | copy-start | bytes 4718596

commit v2 on v1

--- a/solution.py
+++ b/solution.py
@@ -1,4 +1,5 @@
 import functools
+import heapq
 
 import jax
 import jax.numpy as jnp
@@ -100,6 +101,10 @@
     return (jnp.stack([result_zero, result_one], axis=0), state_two)
 
 
+PARTS = 3
+LATENCY, APPLY, GRAD, ADD = 2.0, 1.2, 2.0, 0.5
+
+
 def dot_nt(a, b):
     return lax.dot_general(a, b, (((1,), (1,)), ((), ())), preferred_element_type=jnp.float32)
 
@@ -109,7 +114,7 @@
 
 
 def fused(
-    shards, heads, hidden, width, rows, factor,
+    shards, heads, hidden, width, rows, factor, parts,
     q_ref, k_ref, v_ref, rate_ref, init_ref, out_ref, final_ref,
     weights, acc, state, stage, landed, gather_send, gather_recv, sum_send, sum_recv,
 ):
@@ -131,24 +136,31 @@
         )
     pl.semaphore_wait(barrier, bits)
 
-    def gather_copy(block, p, h):
+    def part_of(c):
+        h, m = c // parts, c % parts
+        size = 3 * width // parts
+        return h, slice(m * size, (m + 1) * size)
+
+    def gather_copy(block, p, c):
+        h, span = part_of(c)
         start = pl.multiple_of(base[p + 1], rows)
-        part = weights.at[block, h, pl.ds(start, spans[p]), :]
+        part = weights.at[block, h, pl.ds(start, spans[p]), span]
         return pltpu.make_async_remote_copy(
             src_ref=part,
             dst_ref=part,
-            send_sem=gather_send.at[block, p, h],
-            recv_sem=gather_recv.at[block, p, h],
+            send_sem=gather_send.at[block, p, c],
+            recv_sem=gather_recv.at[block, p, c],
             device_id={"tok": partner[p]},
             device_id_type=pl.DeviceIdType.MESH,
         )
 
-    def sum_copy(block, p, h):
+    def sum_copy(block, p, c):
+        h, span = part_of(c)
         return pltpu.make_async_remote_copy(
-            src_ref=stage.at[block, h, pl.ds(offset[p], spans[p]), :],
-            dst_ref=landed.at[block, h, pl.ds(offset[p], spans[p]), :],
-            send_sem=sum_send.at[block, p, h],
-            recv_sem=sum_recv.at[block, p, h],
+            src_ref=stage.at[block, h, pl.ds(offset[p], spans[p]), span],
+            dst_ref=landed.at[block, h, pl.ds(offset[p], spans[p]), span],
+            send_sem=sum_send.at[block, p, c],
+            recv_sem=sum_recv.at[block, p, c],
             device_id={"tok": partner[p]},
             device_id_type=pl.DeviceIdType.MESH,
         )
@@ -183,28 +195,29 @@
         gated = (active * second).astype(jnp.bfloat16)
         delta_one = (back * second * sigma * (1.0 + first * (1.0 - sigma))).astype(jnp.bfloat16)
         delta_three = (back * active).astype(jnp.bfloat16)
-        acc[h, :, columns(0)] = dot_nn(delta_one, k)
-        acc[h, :, columns(1)] = dot_nn(delta_three, k)
-        acc[h, :, columns(2)] = dot_nn(gated, scaled)
-
-    def send_sum(block, p, h):
+        for m, left, right in ((0, delta_one, k), (1, delta_three, k), (2, gated, scaled)):
+            acc[h, :, columns(m)] = dot_nn(left, right)
+
+    def send_sum(block, p, c):
+        h, span = part_of(c)
         away = pl.multiple_of(base[p] + (1 - bit[p]) * spans[p], rows)
-        total = acc[h, pl.ds(away, spans[p]), :]
+        total = acc[h, pl.ds(away, spans[p]), span]
         if p > 0:
             before = pl.multiple_of(offset[p - 1] + (1 - bit[p]) * spans[p], rows)
-            total = total + landed[block, h, pl.ds(before, spans[p]), :].astype(jnp.float32)
-        stage[block, h, offset[p] : offset[p] + spans[p], :] = total.astype(jnp.bfloat16)
-        sum_copy(block, p, h).start()
+            total = total + landed[block, h, pl.ds(before, spans[p]), span].astype(jnp.float32)
+        stage[block, h, offset[p] : offset[p] + spans[p], span] = total.astype(jnp.bfloat16)
+        sum_copy(block, p, c).start()
         if p > 0:
             keep = pl.multiple_of(base[p + 1], rows)
             before = pl.multiple_of(offset[p - 1] + bit[p] * spans[p], rows)
-            acc[h, pl.ds(keep, spans[p]), :] = acc[h, pl.ds(keep, spans[p]), :] + landed[
-                block, h, pl.ds(before, spans[p]), :
+            acc[h, pl.ds(keep, spans[p]), span] = acc[h, pl.ds(keep, spans[p]), span] + landed[
+                block, h, pl.ds(before, spans[p]), span
             ].astype(jnp.float32)
 
-    def renorm_head(block, h):
+    def renorm_part(block, c):
         last = bits - 1
-        for m, scale in enumerate((wide, wide, deep)):
+        h = c // parts
+        for m in range(c % parts * 3 // parts, (c % parts + 1) * 3 // parts):
             grad = acc[h, pl.ds(own, rows), columns(m)] + landed[
                 block, h, offset[last] : offset[last] + rows, columns(m)
             ].astype(jnp.float32)
@@ -212,7 +225,7 @@
                 old = init_ref[h, :, columns(m)].astype(jnp.float32)
             else:
                 old = state[h, :, columns(m)]
-            moved = old + (factor * scale) * grad
+            moved = old + (factor * (deep if m == 2 else wide)) * grad
             old_norm = jnp.sqrt(jnp.sum(old * old, axis=1, keepdims=True))
             new_norm = jnp.sqrt(jnp.sum(moved * moved, axis=1, keepdims=True) + 1e-06)
             fresh = moved * (old_norm / new_norm)
@@ -222,59 +235,70 @@
             else:
                 final_ref[h, :, columns(m)] = fresh
 
-    def gather_step(block, step, h):
-        p = bits - 1 - step
-        gather_copy(block, p, h).wait_recv()
-        if p > 0:
-            gather_copy(block, p - 1, h).start()
+    piece = rows * 3 * width * 2 / parts
+    RATES = (300e3, 50e3, 50e3)
+    free = [0.0] * bits
+    landing = []
+    clock = 0.0
+    count = 0
+    todo = []
+    missing = {}
+
+    def issue(kind, block, p, c):
+        nonlocal count
+        link = min(p, 2)
+        blocks = spans[p] // rows * (2 if p == bits - 1 and p > 1 else 1)
+        free[link] = max(free[link], clock) + piece * blocks / RATES[link]
+        heapq.heappush(landing, (free[link] + LATENCY, count, kind, block, p, c))
+        count += 1
 
     for h in range(heads):
         weights[0, h, pl.ds(own, rows), :] = init_ref[h]
-        gather_copy(0, bits - 1, h).start()
-    for turn in range(heads + bits - 1):
-        for step in range(bits - 1, -1, -1):
-            h = turn - step
-            if 0 <= h < heads:
-                gather_step(0, step, h)
-                if step == bits - 1:
-                    gradient_head(0, h)
-                    send_sum(0, 0, h)
-    for turn in range(heads + bits - 1):
-        for p in range(bits - 1, -1, -1):
-            h = turn - p
-            if 0 <= h < heads:
-                sum_copy(0, p, h).wait_recv()
-                if p < bits - 1:
-                    send_sum(0, p + 1, h)
-                else:
-                    renorm_head(0, h)
-                    gather_copy(1, bits - 1, h).start()
-        if turn < heads:
-            apply_head(0, turn)
-    for turn in range(heads + bits - 1):
-        for step in range(bits - 1, -1, -1):
-            h = turn - step
-            if 0 <= h < heads:
-                gather_step(1, step, h)
-                if step == bits - 1:
-                    gradient_head(1, h)
-                    send_sum(1, 0, h)
-    for turn in range(heads + bits - 1):
-        for p in range(bits - 1, -1, -1):
-            h = turn - p
-            if 0 <= h < heads:
-                sum_copy(1, p, h).wait_recv()
-                if p < bits - 1:
-                    send_sum(1, p + 1, h)
-                else:
-                    renorm_head(1, h)
-        if turn < heads:
-            apply_head(1, turn)
+        for c in range(h * parts, (h + 1) * parts):
+            gather_copy(0, bits - 1, c).start()
+            issue("gather", 0, bits - 1, c)
+    while landing:
+        if todo and landing[0][0] > clock + APPLY * 0.5:
+            apply_head(*todo.pop(0))
+            clock += APPLY
+            continue
+        at, _, kind, block, p, c = heapq.heappop(landing)
+        clock = max(clock, at)
+        h = c // parts
+        if kind == "gather":
+            gather_copy(block, p, c).wait_recv()
+            if p > 0:
+                gather_copy(block, p - 1, c).start()
+                issue("gather", block, p - 1, c)
+            else:
+                missing[block, h] = missing.get((block, h), parts) - 1
+                if missing[block, h] == 0:
+                    gradient_head(block, h)
+                    clock += GRAD
+                    for c in range(h * parts, (h + 1) * parts):
+                        send_sum(block, 0, c)
+                        clock += ADD / parts
+                        issue("sum", block, 0, c)
+                    todo.append((block, h))
+        else:
+            sum_copy(block, p, c).wait_recv()
+            if p < bits - 1:
+                send_sum(block, p + 1, c)
+                clock += ADD / parts / (1 << p)
+                issue("sum", block, p + 1, c)
+            else:
+                renorm_part(block, c)
+                clock += 0.3 / parts
+                if block == 0:
+                    gather_copy(1, bits - 1, c).start()
+                    issue("gather", 1, bits - 1, c)
+    for item in todo:
+        apply_head(*item)
     for block in range(2):
         for p in range(bits):
-            for h in range(heads):
-                gather_copy(block, p, h).wait_send()
-                sum_copy(block, p, h).wait_send()
+            for c in range(heads * parts):
+                gather_copy(block, p, c).wait_send()
+                sum_copy(block, p, c).wait_send()
 
 
 def per_device(queries, keys, values, rates, fast_init):
@@ -291,7 +315,7 @@
     start = fast_init.reshape(rows, 3, heads, width).transpose(2, 0, 1, 3).reshape(heads, rows, 3 * width)
     vmem = pl.BlockSpec(memory_space=pltpu.VMEM)
     outputs, final = pl.pallas_call(
-        functools.partial(fused, shards, heads, hidden, width, rows, factor),
+        functools.partial(fused, shards, heads, hidden, width, rows, factor, PARTS),
         out_shape=(
             jax.ShapeDtypeStruct((blocks, tokens, features), jnp.bfloat16),
             jax.ShapeDtypeStruct((heads, rows, 3 * width), jnp.float32),
@@ -304,10 +328,10 @@
             pltpu.VMEM((heads, rows, 3 * width), jnp.float32),
             pltpu.VMEM((2, heads, hidden - rows, 3 * width), jnp.bfloat16),
             pltpu.VMEM((2, heads, hidden - rows, 3 * width), jnp.bfloat16),
-            pltpu.SemaphoreType.DMA((2, bits, heads)),
-            pltpu.SemaphoreType.DMA((2, bits, heads)),
-            pltpu.SemaphoreType.DMA((2, bits, heads)),
-            pltpu.SemaphoreType.DMA((2, bits, heads)),
+            pltpu.SemaphoreType.DMA((2, bits, heads * PARTS)),
+            pltpu.SemaphoreType.DMA((2, bits, heads * PARTS)),
+            pltpu.SemaphoreType.DMA((2, bits, heads * PARTS)),
+            pltpu.SemaphoreType.DMA((2, bits, heads * PARTS)),
         ],
         compiler_params=pltpu.CompilerParams(
             collective_id=0, has_side_effects=True, vmem_limit_bytes=52 * 1024 * 1024

time: 139 us -> 114 us (0.82)
  Pallas kernels: 133 us -> 108 us
    pallas_call x1, Pallas kernels: 133 us -> 108 us  [per_device(): pl.pallas_call(functools.partial(fused, shards, heads, hidden, width, row...]
where the time goes in v2:
time: 114 us; the launch traced here: 113 us
  Pallas kernels  108 us (95%)
  local copies, waits for them, and re-layouts  5.04 us (4%)
    pallas_call x1, Pallas kernels, per_device(): pl.pallas_call(functools.partial(fused, shards, heads, hidden, width, row...  108 us

profile of v2, /device:TPU:0, one launch (start us, length us, event | category | flops | bytes accessed | tf_op | source)
XLA Modules:
  0.0 113.3 jit_solution(998933801123952725)
XLA Ops:
  0.6 0.8 copy.12
  1.5 1.1 reshape.16
  2.5 0.2 copy.16
  2.7 0.3 reshape.17.init_ref
  3.0 107.6 %shard_map.68 = (bf16[2,192,2048]{2,1,0:T(8,128)(2,1)}, f32[4,16,1536]{2,1,0:T(8,128)S(1)}) custom-call(bf16[2,192,2048]{2,1,0:T(8,128)(2,1)} %q_ref.1, bf16[2,192,2048]{2,1,0:T(8,128)(2,1)} %k_ref.1, bf16[2,192,2048]{2,1,0:T(8,128)(2,1)} %v_ref.1, f32[2,192,4]{2,1,0:T(8,128)S(1)} %bitcast.9, bf16[4,16,1536]{2,1,0:T(8,128)(2,1)S(1)} %reshape.17.init_ref), custom_call_target="tpu_custom_call" | custom-call | tf_op jit(solution)/shard_map/pallas_call | solution.py:317
  110.6 0.0 copy-start
  110.6 0.3 reshape.18
  110.9 0.3 copy.14
  111.2 1.0 reshape.19
  112.2 0.0 copy-done
  112.2 1.1 %copy.18 = bf16[2,192,2048]{2,1,0:T(8,128)(2,1)} copy(bf16[2,192,2048]{2,1,0:T(8,128)(2,1)S(1)} %copy-done) | data formatting | bytes 3145728
Async XLA Ops:
  110.6 1.6 %copy-start = (bf16[2,192,2048]{2,1,0:T(8,128)(2,1)S(1)}, bf16[2,192,2048]{2,1,0:T(8,128)(2,1)}, u32[]{:S(2)}) copy-start(bf16[2,192,2048]{2,1,0:T(8,128)(2,1)} %get-tuple-element.8) | copy-start | bytes 4718596

commit v3 on v2

--- a/solution.py
+++ b/solution.py
@@ -115,8 +115,9 @@
 
 def fused(
     shards, heads, hidden, width, rows, factor, parts,
-    q_ref, k_ref, v_ref, rate_ref, init_ref, out_ref, final_ref,
-    weights, acc, state, stage, landed, gather_send, gather_recv, sum_send, sum_recv,
+    q_hbm, k_hbm, v_hbm, rate_ref, init_ref, out_ref, final_ref,
+    q_ref, k_ref, v_ref, load_sem, weights, acc, state, stage, landed, gather_send, gather_recv, sum_send, sum_recv,
+    pair_send, pair_recv,
 ):
     me = lax.axis_index("tok")
     bits = shards.bit_length() - 1
@@ -129,12 +130,20 @@
     own = pl.multiple_of(base[bits], rows)
     offset = [sum(spans[:p]) for p in range(bits)]
 
+    paired = lax.axis_size("groups") == 2 and heads >= 2
+    group = lax.axis_index("groups")
+    pair = (heads - 2, heads - 1) if paired else ()
+
     barrier = pltpu.get_barrier_semaphore()
+    if paired:
+        pl.semaphore_signal(
+            barrier, inc=1, device_id={"groups": 1 - group}, device_id_type=pl.DeviceIdType.MESH
+        )
     for p in range(bits):
         pl.semaphore_signal(
             barrier, inc=1, device_id={"tok": partner[p]}, device_id_type=pl.DeviceIdType.MESH
         )
-    pl.semaphore_wait(barrier, bits)
+    pl.semaphore_wait(barrier, bits + int(paired))
 
     def part_of(c):
         h, m = c // parts, c % parts
@@ -143,6 +152,8 @@
 
     def gather_copy(block, p, c):
         h, span = part_of(c)
+        if block == 0 and h in pair:
+            h = heads - 2 + group if h == heads - 2 else heads - 1 - group
         start = pl.multiple_of(base[p + 1], rows)
         part = weights.at[block, h, pl.ds(start, spans[p]), span]
         return pltpu.make_async_remote_copy(
@@ -151,6 +162,18 @@
             send_sem=gather_send.at[block, p, c],
             recv_sem=gather_recv.at[block, p, c],
             device_id={"tok": partner[p]},
+            device_id_type=pl.DeviceIdType.MESH,
+        )
+
+    def pair_copy(c):
+        h, span = part_of(c)
+        part = weights.at[0, heads - 2 + group, pl.ds(pl.multiple_of(base[1], rows), spans[0]), span]
+        return pltpu.make_async_remote_copy(
+            src_ref=part,
+            dst_ref=part,
+            send_sem=pair_send.at[c % parts],
+            recv_sem=pair_recv.at[c % parts],
+            device_id={"groups": 1 - group},
             device_id_type=pl.DeviceIdType.MESH,
         )
 
@@ -236,8 +259,8 @@
                 final_ref[h, :, columns(m)] = fresh
 
     piece = rows * 3 * width * 2 / parts
-    RATES = (300e3, 50e3, 50e3)
-    free = [0.0] * bits
+    RATES = (300e3, 50e3, 50e3, 50e3)
+    free = [0.0] * 4
     landing = []
     clock = 0.0
     count = 0
@@ -246,17 +269,24 @@
 
     def issue(kind, block, p, c):
         nonlocal count
-        link = min(p, 2)
+        link = 3 if kind == "pair" else min(p, 2)
         blocks = spans[p] // rows * (2 if p == bits - 1 and p > 1 else 1)
         free[link] = max(free[link], clock) + piece * blocks / RATES[link]
         heapq.heappush(landing, (free[link] + LATENCY, count, kind, block, p, c))
         count += 1
 
-    for h in range(heads):
-        weights[0, h, pl.ds(own, rows), :] = init_ref[h]
+    for h in list(pair[:1]) + [h for h in range(heads) if h not in pair]:
+        source = heads - 2 + group if h in pair else h
+        weights[0, source, pl.ds(own, rows), :] = init_ref[source]
         for c in range(h * parts, (h + 1) * parts):
             gather_copy(0, bits - 1, c).start()
             issue("gather", 0, bits - 1, c)
+    loads = [
+        pltpu.make_async_copy(source, target, load_sem.at[i])
+        for i, (source, target) in enumerate(((k_hbm, k_ref), (v_hbm, v_ref), (q_hbm, q_ref)))
+    ]
+    for load in loads:
+        load.start()
     while landing:
         if todo and landing[0][0] > clock + APPLY * 0.5:
             apply_head(*todo.pop(0))
@@ -265,21 +295,33 @@
         at, _, kind, block, p, c = heapq.heappop(landing)
         clock = max(clock, at)
         h = c // parts
-        if kind == "gather":
+        if kind == "pair":
+            pair_copy(c).wait_recv()
+            gather_copy(0, 0, c + parts).start()
+            issue("gather", 0, 0, c + parts)
+        elif kind == "gather":
             gather_copy(block, p, c).wait_recv()
+            if p == 1 and block == 0 and h in pair:
+                pair_copy(c).start()
+                issue("pair", 0, 0, c)
             if p > 0:
                 gather_copy(block, p - 1, c).start()
                 issue("gather", block, p - 1, c)
             else:
-                missing[block, h] = missing.get((block, h), parts) - 1
-                if missing[block, h] == 0:
-                    gradient_head(block, h)
-                    clock += GRAD
-                    for c in range(h * parts, (h + 1) * parts):
-                        send_sum(block, 0, c)
-                        clock += ADD / parts
-                        issue("sum", block, 0, c)
-                    todo.append((block, h))
+                ready = pair if block == 0 and h in pair else (h,)
+                missing[block, ready] = missing.get((block, ready), parts * len(ready)) - 1
+                if missing[block, ready] == 0:
+                    for load in loads:
+                        load.wait()
+                    loads = []
+                    for h in ready:
+                        gradient_head(block, h)
+                        clock += GRAD
+                        for c in range(h * parts, (h + 1) * parts):
+                            send_sum(block, 0, c)
+                            clock += ADD / parts
+                            issue("sum", block, 0, c)
+                        todo.append((block, h))
         else:
             sum_copy(block, p, c).wait_recv()
             if p < bits - 1:
@@ -297,8 +339,12 @@
     for block in range(2):
         for p in range(bits):
             for c in range(heads * parts):
-                gather_copy(block, p, c).wait_send()
+                if block or not p or c // parts not in pair[1:]:
+                    gather_copy(block, p, c).wait_send()
                 sum_copy(block, p, c).wait_send()
+    if paired:
+        for m in range(parts):
+            pair_copy((heads - 2) * parts + m).wait_send()
 
 
 def per_device(queries, keys, values, rates, fast_init):
@@ -320,9 +366,13 @@
             jax.ShapeDtypeStruct((blocks, tokens, features), jnp.bfloat16),
             jax.ShapeDtypeStruct((heads, rows, 3 * width), jnp.float32),
         ),
-        in_specs=[vmem] * 5,
+        in_specs=[pl.BlockSpec(memory_space=pl.ANY)] * 3 + [vmem] * 2,
         out_specs=(vmem, vmem),
         scratch_shapes=[
+            pltpu.VMEM((blocks, tokens, features), jnp.bfloat16),
+            pltpu.VMEM((blocks, tokens, features), jnp.bfloat16),
+            pltpu.VMEM((blocks, tokens, features), jnp.bfloat16),
+            pltpu.SemaphoreType.DMA((3,)),
             pltpu.VMEM((2, heads, hidden, 3 * width), jnp.bfloat16),
             pltpu.VMEM((heads, hidden, 3 * width), jnp.float32),
             pltpu.VMEM((heads, rows, 3 * width), jnp.float32),
@@ -332,6 +382,8 @@
             pltpu.SemaphoreType.DMA((2, bits, heads * PARTS)),
             pltpu.SemaphoreType.DMA((2, bits, heads * PARTS)),
             pltpu.SemaphoreType.DMA((2, bits, heads * PARTS)),
+            pltpu.SemaphoreType.DMA((PARTS,)),
+            pltpu.SemaphoreType.DMA((PARTS,)),
         ],
         compiler_params=pltpu.CompilerParams(
             collective_id=0, has_side_effects=True, vmem_limit_bytes=52 * 1024 * 1024

time: 114 us -> 108 us (0.947)
  Pallas kernels: 108 us -> 102 us
    pallas_call x1, Pallas kernels: 108 us -> 102 us  [per_device(): pl.pallas_call(functools.partial(fused, shards, heads, hidden, width, row...]
where the time goes in v3:
time: 108 us
  Pallas kernels  102 us (94%)
  local copies, waits for them, and re-layouts  5.04 us (5%)
    pallas_call x1, Pallas kernels, per_device(): pl.pallas_call(functools.partial(fused, shards, heads, hidden, width, row...  102 us

profile of v3, /device:TPU:0, one launch (start us, length us, event | category | flops | bytes accessed | tf_op | source)
XLA Modules:
  0.0 107.7 jit_solution(17614447232260118145)
XLA Ops:
  0.6 0.8 copy.12
  1.5 1.1 reshape.16
  2.5 0.2 copy.16
  2.7 0.3 reshape.17.init_ref
  3.0 102.0 %shard_map.68 = (bf16[2,192,2048]{2,1,0:T(8,128)(2,1)}, f32[4,16,1536]{2,1,0:T(8,128)S(1)}) custom-call(bf16[2,192,2048]{2,1,0:T(8,128)(2,1)} %q_hbm.1, bf16[2,192,2048]{2,1,0:T(8,128)(2,1)} %k_hbm.1, bf16[2,192,2048]{2,1,0:T(8,128)(2,1)} %v_hbm.1, f32[2,192,4]{2,1,0:T(8,128)S(1)} %bitcast.9, bf16[4,16,1536]{2,1,0:T(8,128)(2,1)S(1)} %reshape.17.init_ref), custom_call_target="tpu_custom_call" | custom-call | tf_op jit(solution)/shard_map/pallas_call | solution.py:363
  104.9 0.0 copy-start
  105.0 0.3 reshape.18
  105.2 0.3 copy.14
  105.5 1.0 reshape.19
  106.5 0.0 copy-done
  106.5 1.1 %copy.18 = bf16[2,192,2048]{2,1,0:T(8,128)(2,1)} copy(bf16[2,192,2048]{2,1,0:T(8,128)(2,1)S(1)} %copy-done) | data formatting | bytes 3145728
Async XLA Ops:
  104.9 1.6 %copy-start = (bf16[2,192,2048]{2,1,0:T(8,128)(2,1)S(1)}, bf16[2,192,2048]{2,1,0:T(8,128)(2,1)}, u32[]{:S(2)}) copy-start(bf16[2,192,2048]{2,1,0:T(8,128)(2,1)} %get-tuple-element.8) | copy-start | bytes 4718596

commit v4 on v3

--- a/solution.py
+++ b/solution.py
@@ -275,7 +275,7 @@
         heapq.heappush(landing, (free[link] + LATENCY, count, kind, block, p, c))
         count += 1
 
-    for h in list(pair[:1]) + [h for h in range(heads) if h not in pair]:
+    for h in [h for h in range(heads) if h not in pair] + list(pair[:1]):
         source = heads - 2 + group if h in pair else h
         weights[0, source, pl.ds(own, rows), :] = init_ref[source]
         for c in range(h * parts, (h + 1) * parts):

time: 108 us -> 107 us (level)
  no operation moved by 1% of the time
where the time goes in v4:
time: 107 us
  Pallas kernels  101 us (94%)
  local copies, waits for them, and re-layouts  5.04 us (5%)
    pallas_call x1, Pallas kernels, per_device(): pl.pallas_call(functools.partial(fused, shards, heads, hidden, width, row...  101 us

profile of v4, /device:TPU:0, one launch (start us, length us, event | category | flops | bytes accessed | tf_op | source)
XLA Modules:
  0.0 106.8 jit_solution(9816991908734984062)
XLA Ops:
  0.6 0.8 copy.12
  1.5 1.1 reshape.16
  2.5 0.2 copy.16
  2.7 0.3 reshape.17.init_ref
  3.0 101.1 %shard_map.68 = (bf16[2,192,2048]{2,1,0:T(8,128)(2,1)}, f32[4,16,1536]{2,1,0:T(8,128)S(1)}) custom-call(bf16[2,192,2048]{2,1,0:T(8,128)(2,1)} %q_hbm.1, bf16[2,192,2048]{2,1,0:T(8,128)(2,1)} %k_hbm.1, bf16[2,192,2048]{2,1,0:T(8,128)(2,1)} %v_hbm.1, f32[2,192,4]{2,1,0:T(8,128)S(1)} %bitcast.9, bf16[4,16,1536]{2,1,0:T(8,128)(2,1)S(1)} %reshape.17.init_ref), custom_call_target="tpu_custom_call" | custom-call | tf_op jit(solution)/shard_map/pallas_call | solution.py:363
  104.1 0.0 copy-start
  104.1 0.3 reshape.18
  104.4 0.3 copy.14
  104.7 1.0 reshape.19
  105.7 0.0 copy-done
  105.7 1.1 %copy.18 = bf16[2,192,2048]{2,1,0:T(8,128)(2,1)} copy(bf16[2,192,2048]{2,1,0:T(8,128)(2,1)S(1)} %copy-done) | data formatting | bytes 3145728
Async XLA Ops:
  104.1 1.6 %copy-start = (bf16[2,192,2048]{2,1,0:T(8,128)(2,1)S(1)}, bf16[2,192,2048]{2,1,0:T(8,128)(2,1)}, u32[]{:S(2)}) copy-start(bf16[2,192,2048]{2,1,0:T(8,128)(2,1)} %get-tuple-element.8) | copy-start | bytes 4718596
